TPU v7x, 512 devices: a whole 4x8x8 slice. The times are simulated.
512 devices in a mesh: ctx: 32 (over y, z_lo), head: 16 (over x, z_hi, core).
Axes of the slice: x: 4, y: 8, z: 8 (z_hi: 2, z_lo: 4; z = z_hi * 4 + z_lo), core: 2. Of those that a mesh axis runs over, the one named last changes fastest.
Arguments:
- queries: bfloat16 [2, 512, 4096], P(None, ('ctx', 'head')), may hold values from -40 to 40
- cache_kv: bfloat16 [32, 2, 512, 4096], P('ctx', None, None, 'head'), may hold values from -24 to 24
- lengths: int32 [32], P('ctx'), may hold values from 64 to 512, as said below
- evict: int32 [1], replicated, may hold values from 0 to 31
- own_kv: bfloat16 [2, 2, 512, 4096], P(None, None, 'ctx', 'head'), may hold values from -6 to 6
- clean_kv: bfloat16 [2, 512, 4096], P(None, 'ctx', 'head'), may hold values from -6 to 6
Outputs:
- attended: bfloat16 [2, 512, 4096], P(None, ('ctx', 'head'))
- new_cache: bfloat16 [32, 2, 512, 4096], P('ctx', None, None, 'head')
Inputs may be any that keep to these rules, and one draw needn't show every extreme that they name: `lengths`: at least one slot is full.
All inputs are finite; a program needn't handle non-finite values.
Results may differ from a plain program's by a relative error of at most 0.0065.
Values may be sent and summed in bfloat16 or wider, within the bound.
No kernel may reach another device: no remote copies, remote signals or barrier semaphores. Data moves between devices by JAX's collectives and lax.ppermute only.
A program may use at most 64 MiB of HBM per device.

v0:
```python
import math

import jax
import jax.numpy as jnp
from jax import lax
from jax.experimental import pallas as pl
from jax.experimental.pallas import tpu as pltpu
from jax.sharding import PartitionSpec as P

HD = 128
PARTS = 4
BACK = 6
EXP2_SCALE = math.log2(math.e) / math.sqrt(HD)
NEG = -1e30
VMEM = pl.BlockSpec(memory_space=pltpu.VMEM)
SMEM = pl.BlockSpec(memory_space=pltpu.SMEM)
NT = (((1,), (1,)), ((), ()))
NN = (((1,), (0,)), ((), ()))


def spread_kernel(q_ref, out_ref, rows):
    count = rows.shape[0]
    for row in range(count):
        group, step, half = row // 4, row // 2 % 2, row % 2
        start = (group * 2 + half) * HD
        rows[row:row + 1, :] = q_ref[step:step + 1, start:start + HD].astype(jnp.float32)
    message = rows[...].astype(out_ref.dtype)
    for dest in range(out_ref.shape[0] // count):
        out_ref[dest * count:(dest + 1) * count, :] = message


def pack_kernel(length_ref, cache_ref, own_ref, clean_ref, pack_ref, copies_ref):
    span, rows = cache_ref.shape[2], clean_ref.shape[1]
    pack_ref[0:span, :] = cache_ref[0, 0]
    pack_ref[span:2 * span, :] = cache_ref[0, 1]
    place = 2 * span
    for step in range(2):
        for index in range(2):
            pack_ref[place:place + rows, :] = own_ref[step, index]
            place += rows
    for index in range(2):
        pack_ref[place:place + rows, :] = clean_ref[index]
        place += rows
    length = length_ref[0]
    lane = lax.broadcasted_iota(jnp.int32, (rows, 2 * HD), 1)
    digits = jnp.where(lane < HD, length // 8, length % 8)
    pack_ref[place:place + rows, :] = digits.astype(jnp.float32).astype(pack_ref.dtype)
    for dest in range(copies_ref.shape[0]):
        copies_ref[dest] = clean_ref[...]


def attend_kernel(length_ref, evict_ref, recv_ref, cache_ref, own_ref, clean_ref, far_ref, out_ref, wide, wide_out):
    span = cache_ref.shape[2]
    rows = clean_ref.shape[1]
    block = recv_ref.shape[0] // PARTS
    me = lax.axis_index("ca") * 2 + lax.axis_index("cb")
    owner = me == evict_ref[0]
    far_owner = (me ^ 1) == evict_ref[0]
    length = length_ref[0]
    wide[...] = recv_ref[...].astype(jnp.float32)
    key = lax.broadcasted_iota(jnp.int32, (1, span), 1)
    lane = lax.broadcasted_iota(jnp.int32, (1, HD), 1)
    tail = 2 * span
    digits = far_ref[tail + 6 * rows:tail + 7 * rows, :].astype(jnp.float32)[0:1]
    far_length = jnp.concatenate([digits[:, :HD] * 8.0 + digits[:, HD:]] * (span // HD), axis=1)
    ones = jnp.ones((span, HD), jnp.bfloat16)
    pad = jnp.zeros((HD - 4 * rows, 2 * HD), jnp.bfloat16)
    for step in range(2):
        limit = length if step == 0 else jnp.where(owner, 0, length)
        bias = jnp.where(key < limit, 0.0, NEG)
        far_bias = jnp.where(key.astype(jnp.float32) < far_length, 0.0, NEG)
        if step == 1:
            far_bias = jnp.where(far_owner, NEG, far_bias)
        extra_bias = jnp.where((lane % (2 * rows) < rows * (1 + step)) & (lane < 4 * rows), 0.0, NEG)
        extra_keys, extra_values = [
            jnp.concatenate(
                [
                    own_ref[step, index],
                    clean_ref[index],
                    far_ref[tail + (2 * step + index) * rows:tail + (2 * step + index + 1) * rows, :],
                    far_ref[tail + (4 + index) * rows:tail + (5 + index) * rows, :],
                    pad,
                ],
                axis=0,
            )
            for index in range(2)
        ]
        stats = jnp.zeros((block, HD), jnp.float32)
        for half in range(2):
            part = step * 2 + half
            lanes = slice(half * HD, (half + 1) * HD)
            query = wide[pl.ds(part, block, stride=PARTS), :].astype(jnp.bfloat16)
            groups = (
                (cache_ref[0, 0, :, lanes], cache_ref[0, 1, :, lanes], bias),
                (far_ref[0:span, lanes], far_ref[span:2 * span, lanes], far_bias),
                (extra_keys[:, lanes], extra_values[:, lanes], extra_bias),
            )
            scores = [
                lax.dot_general(query, keys, NT, preferred_element_type=jnp.float32) + mask for keys, _, mask in groups
            ]
            top = jnp.max(scores[0], axis=1, keepdims=True)
            for score in scores[1:]:
                top = jnp.maximum(top, jnp.max(score, axis=1, keepdims=True))
            top = jnp.ceil(top)
            accum = jnp.zeros((block, 2 * HD), jnp.float32)
            for score, (_, values, _) in zip(scores, groups):
                weights = jnp.exp2((score - top) * EXP2_SCALE).astype(jnp.bfloat16)
                values = jnp.concatenate([values, ones[:values.shape[0]]], axis=1)
                accum = accum + lax.dot_general(weights, values, NN, preferred_element_type=jnp.float32)
            wide_out[pl.ds(half * 2 + step, block, stride=BACK), :] = accum[:, :HD]
            total = accum[:, HD:]
            top = jnp.broadcast_to(top, (block, HD))
            top_hi = top.astype(jnp.bfloat16).astype(jnp.float32)
            total_hi = total.astype(jnp.bfloat16).astype(jnp.float32)
            for place, value in enumerate((top_hi, top - top_hi, total_hi, total - total_hi)):
                stats = jnp.where(lane == 32 * place + half, value, stats)
        wide_out[pl.ds(4 + step, block, stride=BACK), :] = stats
    out_ref[...] = wide_out[...].astype(jnp.bfloat16)


def combine_kernel(recv_ref, out_ref, wide):
    groups = out_ref.shape[1] // (2 * HD)
    senders = recv_ref.shape[0] // BACK
    devices = senders // groups
    wide[...] = recv_ref[...].astype(jnp.float32)

    def rows_of(place):
        return wide[pl.ds(place, senders, stride=BACK), :].reshape(devices, groups, HD)

    for step in range(2):
        stats = rows_of(4 + step)
        for half in range(2):
            local = stats[:, :, half:half + 1] + stats[:, :, 32 + half:33 + half]
            total = stats[:, :, 64 + half:65 + half] + stats[:, :, 96 + half:97 + half]
            top = jnp.max(local, axis=0, keepdims=True)
            scale = jnp.exp2((local - top) * EXP2_SCALE)
            whole = jnp.sum(scale * total, axis=0)
            result = jnp.sum(scale * rows_of(half * 2 + step), axis=0) / whole
            for group in range(groups):
                begin = (group * 2 + half) * HD
                out_ref[step:step + 1, begin:begin + HD] = result[group:group + 1].astype(jnp.bfloat16)


def renew_kernel(evict_ref, near_ref, far_ref, cache_ref, new_ref):
    devices, _, rows, _ = near_ref.shape
    parity = lax.axis_index("cb")
    owner = lax.axis_index("ca") * 2 + parity == evict_ref[0]

    @pl.when(owner)
    def _():
        for ref, kind in ((near_ref, parity), (far_ref, 1 - parity)):
            for device in range(devices):
                place = pl.ds(pl.multiple_of((device * 2 + kind) * rows, rows), rows)
                for index in range(2):
                    new_ref[0, index, place, :] = ref[device, index]

    @pl.when(jnp.logical_not(owner))
    def _():
        new_ref[...] = cache_ref[...]


def call(kernel, out_shape, in_specs, scratch=(), name=None):
    several = isinstance(out_shape, tuple)
    return pl.pallas_call(
        kernel,
        out_shape=out_shape,
        in_specs=in_specs,
        out_specs=(VMEM,) * len(out_shape) if several else VMEM,
        scratch_shapes=list(scratch),
        compiler_params=pltpu.CompilerParams(vmem_limit_bytes=40 * 1024 * 1024),
        name=name,
    )


def body(queries, cache_kv, lengths, evict, own_kv, clean_kv):
    steps, _, features = queries.shape
    _, kinds, span, width = cache_kv.shape
    pairs = lax.axis_size("ca")
    groups = lax.axis_size("head")
    rows = clean_kv.shape[1]
    tokens = pairs * groups
    bf16, f32 = jnp.bfloat16, jnp.float32
    shape = jax.ShapeDtypeStruct
    swap = [(0, 1), (1, 0)]
    pack, copies = call(
        pack_kernel,
        (shape((2 * span + 7 * rows, width), bf16), shape((pairs,) + clean_kv.shape, bf16)),
        [SMEM] + [VMEM] * 3,
        name="pack",
    )(lengths, cache_kv, own_kv, clean_kv)
    far = lax.ppermute(pack, "cb", swap)
    message = call(
        spread_kernel,
        shape((tokens * PARTS, HD), bf16),
        [VMEM],
        [pltpu.VMEM((groups * PARTS, HD), f32)],
        name="spread_queries",
    )(queries.reshape(steps, features))
    recv = lax.all_to_all(
        message.reshape(tokens, PARTS, HD), ("ca", "head"), split_axis=0, concat_axis=0, tiled=True
    ).reshape(tokens * PARTS, HD)
    parts = call(
        attend_kernel,
        shape((tokens * BACK, HD), bf16),
        [SMEM, SMEM] + [VMEM] * 5,
        [pltpu.VMEM((tokens * PARTS, HD), f32), pltpu.VMEM((tokens * BACK, HD), f32)],
        name="attend",
    )(lengths, evict, recv, cache_kv, own_kv, clean_kv, far)
    _, copies = lax.optimization_barrier((recv, copies))
    near = lax.all_to_all(copies, "ca", split_axis=0, concat_axis=0, tiled=True)
    parts, near = lax.optimization_barrier((parts, near))
    back = lax.all_to_all(
        parts.reshape(tokens * BACK // 2, 2, HD), ("ca", "head"), split_axis=0, concat_axis=0, tiled=True
    ).reshape(tokens * BACK, HD)
    attended = call(
        combine_kernel,
        shape((steps, features), bf16),
        [VMEM],
        [pltpu.VMEM((tokens * BACK, HD), f32)],
        name="combine",
    )(back)
    other = lax.ppermute(near, "cb", swap)
    new_cache = call(renew_kernel, shape(cache_kv.shape, bf16), [SMEM] + [VMEM] * 3, name="renew_cache")(
        evict, near, other, cache_kv
    )
    return (attended.reshape(steps, 1, features), new_cache)


def solution(mesh):
    ctx, heads = mesh.devices.shape
    halves = jax.sharding.Mesh(mesh.devices.reshape(ctx // 2, 2, heads), ("ca", "cb", "head"))
    ctx = ("ca", "cb")
    in_specs = (
        P(None, ctx + ("head",), None),
        P(ctx, None, None, "head"),
        P(ctx),
        P(),
        P(None, None, ctx, "head"),
        P(None, ctx, "head"),
    )
    out_specs = (P(None, ctx + ("head",), None), P(ctx, None, None, "head"))
    return jax.shard_map(body, mesh=halves, in_specs=in_specs, out_specs=out_specs, check_vma=False)
```

profile of v0, /device:TPU:1, one launch (start us, length us, event | category | flops | bytes accessed | tf_op | source)
XLA Modules:
  0.0 89.5 jit_solution(2041579657639938272)
XLA Ops:
  0.6 0.0 copy-start
  0.6 0.0 copy-start.3
  0.6 0.8 copy-done.3
  1.4 0.7 spread_queries.1
  2.2 0.0 copy-start.1
  2.2 0.0 copy-start.2
  2.2 22.5 %all-to-all-start = ((bf16[256,4,128]{2,1,0:T(4,128)(2,1)}), bf16[256,4,128]{2,1,0:T(4,128)(2,1)S(1)}, u32[]{:S(2)}, u32[]{:S(2)}) async-start(bf16[256,4,128]{2,1,0:T(4,128)(2,1)} %bitcast.1), calls=%async_computation | async-start | bytes 524288 | tf_op jit(solution)/shard_map/all_to_all | solution.py:199
  25.3 0.0 copy-done
  25.3 0.0 copy-done.1
  25.4 0.0 copy-done.2
  25.4 0.8 pack.1
  26.1 3.1 %collective-permute-start = (bf16[1136,256]{1,0:T(8,128)(2,1)S(1)}, bf16[1136,256]{1,0:T(8,128)(2,1)S(1)}, u32[]{:S(2)}, u32[]{:S(2)}) collective-permute-start(bf16[1136,256]{1,0:T(8,128)(2,1)S(1)} %get-tuple-element.7), channel_id=1, source_target_pairs={{0,16},{16,0},{1,17},{17,1},{2,18},{18,2},{3,19},{19,3},{4,20},{20... | collective-permute-start | bytes 1744904 | tf_op jit(solution)/shard_map/ppermute | solution.py:191
  29.2 13.5 %all-to-all-done = bf16[256,4,128]{2,1,0:T(4,128)(2,1)S(1)} async-done(((bf16[256,4,128]{2,1,0:T(4,128)(2,1)}), bf16[256,4,128]{2,1,0:T(4,128)(2,1)S(1)}, u32[]{:S(2)}, u32[]{:S(2)}) %all-to-all-start) | async-done | bytes 262176 | tf_op jit(solution)/shard_map/all_to_all | solution.py:199
  42.7 3.5 %all-to-all-start.1 = ((bf16[16,2,16,256]{3,2,1,0:T(8,128)(2,1)}), bf16[16,2,16,256]{3,2,1,0:T(8,128)(2,1)S(1)}, u32[]{:S(2)}, u32[]{:S(2)}) async-start(bf16[16,2,16,256]{3,2,1,0:T(8,128)(2,1)} %get-tuple-element.9), calls=%async_computation.1 | async-start | bytes 524288 | tf_op jit(solution)/shard_map/all_to_all | solution.py:210
  46.9 0.0 collective-permute-done.far_ref
  46.9 3.1 %attend.1 = bf16[1536,128]{1,0:T(8,128)(2,1)} custom-call(s32[1]{0:T(128)S(6)} %copy.8.length_ref, s32[1]{0:T(128)S(6)} %copy.9.evict_ref, bf16[1024,128]{1,0:T(8,128)(2,1)S(1)} %bitcast.7, bf16[1,2,512,256]{3,2,1,0:T(8,128)(2,1)S(1)} %copy-done, bf16[2,2,16,256]{3,2,1,0:T(8,128)(2,1)S(1)} %copy-done.1, bf16[2,16,256]{2,1,0:T(8,128)(2,1)S(1)} %copy-done.2, ...), custom_call_target="tpu_custom_call" | custom-call | tf_op jit(solution)/shard_map/attend/pallas_call | solution.py:202
  50.0 9.3 %all-to-all-done.1.near_ref = bf16[16,2,16,256]{3,2,1,0:T(8,128)(2,1)S(1)} async-done(((bf16[16,2,16,256]{3,2,1,0:T(8,128)(2,1)}), bf16[16,2,16,256]{3,2,1,0:T(8,128)(2,1)S(1)}, u32[]{:S(2)}, u32[]{:S(2)}) %all-to-all-start.1) | async-done | bytes 262176 | tf_op jit(solution)/shard_map/all_to_all | solution.py:210
  59.3 8.3 %all-to-all-start.2 = ((bf16[768,2,128]{2,1,0:T(2,128)(2,1)}), bf16[768,2,128]{2,1,0:T(2,128)(2,1)S(1)}, u32[]{:S(2)}, u32[]{:S(2)}) async-start(bf16[768,2,128]{2,1,0:T(2,128)(2,1)} %bitcast.3), calls=%async_computation.2 | async-start | bytes 786432 | tf_op jit(solution)/shard_map/all_to_all | solution.py:212
  67.6 2.9 %collective-permute-start.1 = (bf16[16,2,16,256]{3,2,1,0:T(8,128)(2,1)S(1)}, bf16[16,2,16,256]{3,2,1,0:T(8,128)(2,1)S(1)}, u32[]{:S(2)}, u32[]{:S(2)}) collective-permute-start(bf16[16,2,16,256]{3,2,1,0:T(8,128)(2,1)S(1)} %all-to-all-done.1.near_ref), channel_id=1, source_target_pairs={{0,16},{16,0},{1,17},{17,1},{2,18},{18,2},{3,19},{19,3},{4,20},{20... | collective-permute-start | bytes 786440 | tf_op jit(solution)/shard_map/ppermute | solution.py:222
  70.5 13.4 %collective-permute-done.1.far_ref = bf16[16,2,16,256]{3,2,1,0:T(8,128)(2,1)S(1)} collective-permute-done((bf16[16,2,16,256]{3,2,1,0:T(8,128)(2,1)S(1)}, bf16[16,2,16,256]{3,2,1,0:T(8,128)(2,1)S(1)}, u32[]{:S(2)}, u32[]{:S(2)}) %collective-permute-start.1) | collective-permute-done | bytes 262176 | tf_op jit(solution)/shard_map/ppermute | solution.py:222
  83.9 0.8 renew_cache.1
  84.7 3.7 %all-to-all-done.2 = bf16[768,2,128]{2,1,0:T(2,128)(2,1)S(1)} async-done(((bf16[768,2,128]{2,1,0:T(2,128)(2,1)}), bf16[768,2,128]{2,1,0:T(2,128)(2,1)S(1)}, u32[]{:S(2)}, u32[]{:S(2)}) %all-to-all-start.2) | async-done | bytes 393248 | tf_op jit(solution)/shard_map/all_to_all | solution.py:212
  88.4 1.2 %combine.1 = bf16[2,4096]{1,0:T(2,128)(2,1)} custom-call(bf16[1536,128]{1,0:T(8,128)(2,1)S(1)} %bitcast.6), custom_call_target="tpu_custom_call" | custom-call | tf_op jit(solution)/shard_map/combine/pallas_call | solution.py:215
Async XLA Ops:
  0.6 24.7 %copy-start = (bf16[1,2,512,256]{3,2,1,0:T(8,128)(2,1)S(1)}, bf16[1,2,512,256]{3,2,1,0:T(8,128)(2,1)}, u32[]{:S(2)}) copy-start(bf16[1,2,512,256]{3,2,1,0:T(8,128)(2,1)} %cache_ref.5) | copy-start | bytes 1572868
  0.6 0.8 copy-start.3
  2.2 23.2 %copy-start.1 = (bf16[2,2,16,256]{3,2,1,0:T(8,128)(2,1)S(1)}, bf16[2,2,16,256]{3,2,1,0:T(8,128)(2,1)}, u32[]{:S(2)}) copy-start(bf16[2,2,16,256]{3,2,1,0:T(8,128)(2,1)} %own_ref.3) | copy-start | bytes 98308
  2.2 23.2 %copy-start.2 = (bf16[2,16,256]{2,1,0:T(8,128)(2,1)S(1)}, bf16[2,16,256]{2,1,0:T(8,128)(2,1)}, u32[]{:S(2)}) copy-start(bf16[2,16,256]{2,1,0:T(8,128)(2,1)} %clean_ref.3) | copy-start | bytes 49156
  2.2 40.5 %all-to-all-start = ((bf16[256,4,128]{2,1,0:T(4,128)(2,1)}), bf16[256,4,128]{2,1,0:T(4,128)(2,1)S(1)}, u32[]{:S(2)}, u32[]{:S(2)}) async-start(bf16[256,4,128]{2,1,0:T(4,128)(2,1)} %bitcast.1), calls=%async_computation | async-start | bytes 524288 | tf_op jit(solution)/shard_map/all_to_all | solution.py:199
  26.1 20.8 %collective-permute-start = (bf16[1136,256]{1,0:T(8,128)(2,1)S(1)}, bf16[1136,256]{1,0:T(8,128)(2,1)S(1)}, u32[]{:S(2)}, u32[]{:S(2)}) collective-permute-start(bf16[1136,256]{1,0:T(8,128)(2,1)S(1)} %get-tuple-element.7), channel_id=1, source_target_pairs={{0,16},{16,0},{1,17},{17,1},{2,18},{18,2},{3,19},{19,3},{4,20},{20... | collective-permute-start | bytes 1744904 | tf_op jit(solution)/shard_map/ppermute | solution.py:191
  42.7 16.5 %all-to-all-start.1 = ((bf16[16,2,16,256]{3,2,1,0:T(8,128)(2,1)}), bf16[16,2,16,256]{3,2,1,0:T(8,128)(2,1)S(1)}, u32[]{:S(2)}, u32[]{:S(2)}) async-start(bf16[16,2,16,256]{3,2,1,0:T(8,128)(2,1)} %get-tuple-element.9), calls=%async_computation.1 | async-start | bytes 524288 | tf_op jit(solution)/shard_map/all_to_all | solution.py:210
  59.3 29.1 %all-to-all-start.2 = ((bf16[768,2,128]{2,1,0:T(2,128)(2,1)}), bf16[768,2,128]{2,1,0:T(2,128)(2,1)S(1)}, u32[]{:S(2)}, u32[]{:S(2)}) async-start(bf16[768,2,128]{2,1,0:T(2,128)(2,1)} %bitcast.3), calls=%async_computation.2 | async-start | bytes 786432 | tf_op jit(solution)/shard_map/all_to_all | solution.py:212
  67.6 16.3 %collective-permute-start.1 = (bf16[16,2,16,256]{3,2,1,0:T(8,128)(2,1)S(1)}, bf16[16,2,16,256]{3,2,1,0:T(8,128)(2,1)S(1)}, u32[]{:S(2)}, u32[]{:S(2)}) collective-permute-start(bf16[16,2,16,256]{3,2,1,0:T(8,128)(2,1)S(1)} %all-to-all-done.1.near_ref), channel_id=1, source_target_pairs={{0,16},{16,0},{1,17},{17,1},{2,18},{18,2},{3,19},{19,3},{4,20},{20... | collective-permute-start | bytes 786440 | tf_op jit(solution)/shard_map/ppermute | solution.py:222
where the time goes:
time: 90 us; the launch traced here: 89.5 us
  starting transfers between devices  40.3 us (45%)
  waiting for transfers between devices  39.9 us (44%)
  Pallas kernels  6.56 us (7%)
  between operations  2.02 us (2%)
    all_to_all x1, starting transfers between devices, body(): lax.all_to_all(message.reshape(tokens, PARTS, HD), ('ca', 'head'), split_...  22.5 us
    all_to_all x1, waiting for transfers between devices, body(): lax.all_to_all(message.reshape(tokens, PARTS, HD), ('ca', 'head'), split_...  13.5 us
    ppermute x1, waiting for transfers between devices, body(): other = lax.ppermute(near, 'cb', swap)  13.4 us
    all_to_all x1, waiting for transfers between devices, body(): near = lax.all_to_all(copies, 'ca', split_axis=0, concat_axis=0, tiled=True)  9.27 us
    all_to_all x1, starting transfers between devices, body(): lax.all_to_all(parts.reshape(tokens * BACK // 2, 2, HD), ('ca', 'head'),...  8.3 us
    all_to_all x1, waiting for transfers between devices, body(): lax.all_to_all(parts.reshape(tokens * BACK // 2, 2, HD), ('ca', 'head'),...  3.71 us
    all_to_all x1, starting transfers between devices, body(): near = lax.all_to_all(copies, 'ca', split_axis=0, concat_axis=0, tiled=True)  3.53 us
    ppermute x1, starting transfers between devices, body(): far = lax.ppermute(pack, 'cb', swap)  3.09 us
  transfers between devices with their start and end apart: 5, of which 4 were waited for; matrix products, arithmetic and copies ran while one was open for 0% of the time, Pallas kernels for 5%

commit v1 on v0

v1 whole, which is shorter than its diff:
```python
import math

import jax
import jax.numpy as jnp
from jax import lax
from jax.experimental import pallas as pl
from jax.experimental.pallas import tpu as pltpu
from jax.sharding import PartitionSpec as P

HD = 128
PARTS = 8
BACK = 10
EXP2_SCALE = math.log2(math.e) / math.sqrt(HD)
NEG = -1e30
VMEM = pl.BlockSpec(memory_space=pltpu.VMEM)
SMEM = pl.BlockSpec(memory_space=pltpu.SMEM)
NT = (((1,), (1,)), ((), ()))
NN = (((1,), (0,)), ((), ()))


def spread_kernel(q_ref, out_ref, rows):
    count = rows.shape[0]
    for row in range(count):
        chip, step, head = row // PARTS, row // 4 % 2, row % 4
        start = (chip * 4 + head) * HD
        rows[row:row + 1, :] = q_ref[step:step + 1, start:start + HD].astype(jnp.float32)
    message = rows[...].astype(out_ref.dtype)
    for dest in range(out_ref.shape[0] // count):
        out_ref[dest * count:(dest + 1) * count, :] = message


def pack_kernel(length_ref, cache_ref, own_ref, clean_ref, pack_ref, copies_ref):
    span, rows = cache_ref.shape[2], clean_ref.shape[1]
    pack_ref[0:span, :] = cache_ref[0, 0]
    pack_ref[span:2 * span, :] = cache_ref[0, 1]
    place = 2 * span
    for step in range(2):
        for index in range(2):
            pack_ref[place:place + rows, :] = own_ref[step, index]
            place += rows
    for index in range(2):
        pack_ref[place:place + rows, :] = clean_ref[index]
        place += rows
    length = length_ref[0]
    lane = lax.broadcasted_iota(jnp.int32, (rows, 2 * HD), 1)
    digits = jnp.where(lane < HD, length // 8, length % 8)
    pack_ref[place:place + rows, :] = digits.astype(jnp.float32).astype(pack_ref.dtype)
    for dest in range(copies_ref.shape[0]):
        copies_ref[dest] = clean_ref[...]


def attend_kernel(evict_ref, recv_ref, pack_ref, far_ref, side_ref, cross_ref, out_ref, wide, wide_out):
    block = recv_ref.shape[0] // PARTS
    rows = 16
    span = (pack_ref.shape[0] - 7 * rows) // 2
    tail = 2 * span
    me = lax.axis_index("ca") * 2 + lax.axis_index("cb")
    core = lax.axis_index("hb")
    owners = [me == evict_ref[0], (me ^ 1) == evict_ref[0]]
    wide[...] = recv_ref[...].astype(jnp.float32)
    key = lax.broadcasted_iota(jnp.int32, (1, span), 1).astype(jnp.float32)
    lane = lax.broadcasted_iota(jnp.int32, (1, HD), 1)
    lengths = []
    for ref in (pack_ref, far_ref):
        digits = ref[tail + 6 * rows:tail + 7 * rows, :].astype(jnp.float32)[0:1]
        lengths.append(jnp.concatenate([digits[:, :HD] * 8.0 + digits[:, HD:]] * (span // HD), axis=1))
    ones = jnp.ones((span, HD), jnp.bfloat16)
    pad = jnp.zeros((HD - 4 * rows, 2 * HD), jnp.bfloat16)
    for step in range(2):
        biases = []
        for length, owner in zip(lengths, owners):
            bias = jnp.where(key < length, 0.0, NEG)
            biases.append(bias if step == 0 else jnp.where(owner, NEG, bias))
        extra_bias = jnp.where((lane % (2 * rows) < rows * (1 + step)) & (lane < 4 * rows), 0.0, NEG)
        stats = jnp.zeros((block, HD), jnp.float32)
        for side, refs in enumerate(((pack_ref, far_ref), (side_ref, cross_ref))):
            extras = []
            for index in range(2):
                pieces = []
                for ref in refs:
                    own = tail + (2 * step + index) * rows
                    clean = tail + (4 + index) * rows
                    pieces += [ref[own:own + rows, :], ref[clean:clean + rows, :]]
                extras.append(jnp.concatenate(pieces + [pad], axis=0))
            for half in range(2):
                head = (core ^ side) * 2 + half
                lanes = slice(half * HD, (half + 1) * HD)
                query = wide[pl.ds(step * 4 + head, block, stride=PARTS), :].astype(jnp.bfloat16)
                groups = [(ref[0:span, lanes], ref[span:2 * span, lanes], bias) for ref, bias in zip(refs, biases)]
                groups.append((extras[0][:, lanes], extras[1][:, lanes], extra_bias))
                scores = [
                    lax.dot_general(query, keys, NT, preferred_element_type=jnp.float32) + mask
                    for keys, _, mask in groups
                ]
                top = jnp.max(scores[0], axis=1, keepdims=True)
                for score in scores[1:]:
                    top = jnp.maximum(top, jnp.max(score, axis=1, keepdims=True))
                top = jnp.ceil(top)
                accum = jnp.zeros((block, 2 * HD), jnp.float32)
                for score, (_, values, _) in zip(scores, groups):
                    weights = jnp.exp2((score - top) * EXP2_SCALE).astype(jnp.bfloat16)
                    values = jnp.concatenate([values, ones[:values.shape[0]]], axis=1)
                    accum = accum + lax.dot_general(weights, values, NN, preferred_element_type=jnp.float32)
                wide_out[pl.ds(head * 2 + step, block, stride=BACK), :] = accum[:, :HD]
                total = accum[:, HD:]
                top = jnp.broadcast_to(top, (block, HD))
                top_hi = top.astype(jnp.bfloat16).astype(jnp.float32)
                total_hi = total.astype(jnp.bfloat16).astype(jnp.float32)
                for place, value in enumerate((top_hi, top - top_hi, total_hi, total - total_hi)):
                    stats = jnp.where(lane == 32 * place + head, value, stats)
        wide_out[pl.ds(8 + step, block, stride=BACK), :] = stats
    out_ref[...] = wide_out[...].astype(jnp.bfloat16)


def combine_kernel(recv_ref, out_ref, wide):
    chips = out_ref.shape[1] // (4 * HD)
    senders = recv_ref.shape[0] // BACK
    devices = senders // chips
    wide[...] = recv_ref[...].astype(jnp.float32)

    def rows_of(place):
        return wide[pl.ds(place, senders, stride=BACK), :].reshape(devices, chips, HD)

    for step in range(2):
        stats = rows_of(8 + step)
        for head in range(4):
            local = stats[:, :, head:head + 1] + stats[:, :, 32 + head:33 + head]
            total = stats[:, :, 64 + head:65 + head] + stats[:, :, 96 + head:97 + head]
            top = jnp.max(local, axis=0, keepdims=True)
            scale = jnp.exp2((local - top) * EXP2_SCALE)
            whole = jnp.sum(scale * total, axis=0)
            result = jnp.sum(scale * rows_of(head * 2 + step), axis=0) / whole
            for chip in range(chips):
                begin = (chip * 4 + head) * HD
                out_ref[step:step + 1, begin:begin + HD] = result[chip:chip + 1].astype(jnp.bfloat16)


def renew_kernel(evict_ref, near_ref, far_ref, cache_ref, new_ref):
    devices, _, rows, _ = near_ref.shape
    parity = lax.axis_index("cb")
    owner = lax.axis_index("ca") * 2 + parity == evict_ref[0]

    @pl.when(owner)
    def _():
        for ref, kind in ((near_ref, parity), (far_ref, 1 - parity)):
            for device in range(devices):
                place = pl.ds(pl.multiple_of((device * 2 + kind) * rows, rows), rows)
                for index in range(2):
                    new_ref[0, index, place, :] = ref[device, index]

    @pl.when(jnp.logical_not(owner))
    def _():
        new_ref[...] = cache_ref[...]


def call(kernel, out_shape, in_specs, scratch=(), name=None):
    several = isinstance(out_shape, tuple)
    return pl.pallas_call(
        kernel,
        out_shape=out_shape,
        in_specs=in_specs,
        out_specs=(VMEM,) * len(out_shape) if several else VMEM,
        scratch_shapes=list(scratch),
        compiler_params=pltpu.CompilerParams(vmem_limit_bytes=40 * 1024 * 1024),
        name=name,
    )


def body(queries, cache_kv, lengths, evict, own_kv, clean_kv):
    steps, _, features = queries.shape
    span, width = cache_kv.shape[2:]
    pairs = lax.axis_size("ca")
    chips = lax.axis_size("ha")
    rows = clean_kv.shape[1]
    tokens = pairs * chips
    bf16, f32 = jnp.bfloat16, jnp.float32
    shape = jax.ShapeDtypeStruct
    swap = [(0, 1), (1, 0)]
    pack, copies = call(
        pack_kernel,
        (shape((2 * span + 7 * rows, width), bf16), shape((pairs,) + clean_kv.shape, bf16)),
        [SMEM] + [VMEM] * 3,
        name="pack",
    )(lengths, cache_kv, own_kv, clean_kv)
    far = lax.ppermute(pack, "cb", swap)
    side = lax.ppermute(pack, "hb", swap)
    cross = lax.ppermute(far, "hb", swap)
    message = call(
        spread_kernel,
        shape((tokens * PARTS, HD), bf16),
        [VMEM],
        [pltpu.VMEM((chips * PARTS, HD), f32)],
        name="spread_queries",
    )(queries.reshape(steps, features))
    recv = lax.all_to_all(
        message.reshape(tokens, PARTS, HD), ("ca", "ha"), split_axis=0, concat_axis=0, tiled=True
    ).reshape(tokens * PARTS, HD)
    parts = call(
        attend_kernel,
        shape((tokens * BACK, HD), bf16),
        [SMEM] + [VMEM] * 5,
        [pltpu.VMEM((tokens * PARTS, HD), f32), pltpu.VMEM((tokens * BACK, HD), f32)],
        name="attend",
    )(evict, recv, pack, far, side, cross)
    _, copies = lax.optimization_barrier((recv, copies))
    near = lax.all_to_all(copies, "ca", split_axis=0, concat_axis=0, tiled=True)
    parts, near = lax.optimization_barrier((parts, near))
    back = lax.all_to_all(
        parts.reshape(tokens * BACK // 2, 2, HD), ("ca", "ha"), split_axis=0, concat_axis=0, tiled=True
    ).reshape(tokens * BACK, HD)
    attended = call(
        combine_kernel,
        shape((steps, features), bf16),
        [VMEM],
        [pltpu.VMEM((tokens * BACK, HD), f32)],
        name="combine",
    )(back)
    other = lax.ppermute(near, "cb", swap)
    new_cache = call(renew_kernel, shape(cache_kv.shape, bf16), [SMEM] + [VMEM] * 3, name="renew_cache")(
        evict, near, other, cache_kv
    )
    return (attended.reshape(steps, 1, features), new_cache)


def solution(mesh):
    ctx, heads = mesh.devices.shape
    split = jax.sharding.Mesh(mesh.devices.reshape(ctx // 2, 2, heads // 2, 2), ("ca", "cb", "ha", "hb"))
    ctx, heads = ("ca", "cb"), ("ha", "hb")
    in_specs = (
        P(None, ctx + heads, None),
        P(ctx, None, None, heads),
        P(ctx),
        P(),
        P(None, None, ctx, heads),
        P(None, ctx, heads),
    )
    out_specs = (P(None, ctx + heads, None), P(ctx, None, None, heads))
    return jax.shard_map(body, mesh=split, in_specs=in_specs, out_specs=out_specs, check_vma=False)
```

time: 90 us -> 85.5 us (0.950)
  the two profiles are of different devices: /device:TPU:1 before, /device:TPU:6 now
where the time goes in v1:
time: 85.5 us; the launch traced here: 84.9 us
  starting transfers between devices  41.6 us (49%)
  waiting for transfers between devices  32.5 us (38%)
  Pallas kernels  6.26 us (7%)
  local copies, waits for them, and re-layouts  2.52 us (3%)
  between operations  2.03 us (2%)
    all_to_all x1, starting transfers between devices, body(): lax.all_to_all(message.reshape(tokens, PARTS, HD), ('ca', 'ha'), split_ax...  18.9 us
    all_to_all x1, waiting for transfers between devices, body(): lax.all_to_all(message.reshape(tokens, PARTS, HD), ('ca', 'ha'), split_ax...  11.7 us
    ppermute x1, waiting for transfers between devices, body(): other = lax.ppermute(near, 'cb', swap)  10.2 us
    all_to_all x1, waiting for transfers between devices, body(): near = lax.all_to_all(copies, 'ca', split_axis=0, concat_axis=0, tiled=True)  8.22 us
    all_to_all x1, starting transfers between devices, body(): lax.all_to_all(parts.reshape(tokens * BACK // 2, 2, HD), ('ca', 'ha'), sp...  8.04 us
    ppermute x1, starting transfers between devices, body(): far = lax.ppermute(pack, 'cb', swap)  4.27 us
    all_to_all x1, starting transfers between devices, body(): near = lax.all_to_all(copies, 'ca', split_axis=0, concat_axis=0, tiled=True)  3.53 us
    pallas_call x1, Pallas kernels, body(): call(attend_kernel, shape((tokens * BACK, HD), bf16), [SMEM] + [VMEM] * 5...  2.83 us
  transfers between devices with their start and end apart: 7, of which 4 were waited for; matrix products, arithmetic and copies ran while one was open for 0% of the time, Pallas kernels for 5%

profile of v1, /device:TPU:6, one launch (start us, length us, event | category | flops | bytes accessed | tf_op | source)
XLA Modules:
  0.0 84.9 jit_solution(3619241448476033394)
XLA Ops:
  1.3 0.0 copy-start
  1.3 1.0 %copy-done = bf16[1,2,512,256]{3,2,1,0:T(8,128)(2,1)S(1)} copy-done((bf16[1,2,512,256]{3,2,1,0:T(8,128)(2,1)S(1)}, bf16[1,2,512,256]{3,2,1,0:T(8,128)(2,1)}, u32[]{:S(2)}) %copy-start) | copy-done | bytes 524312
  2.3 0.0 copy-start.2
  2.3 0.8 copy-done.2
  3.1 0.0 copy-start.4
  3.1 0.7 copy-done.4
  3.8 0.0 copy-start.3
  3.8 0.7 pack.1
  4.5 4.3 %collective-permute-start = (bf16[1136,256]{1,0:T(8,128)(2,1)S(1)}, bf16[1136,256]{1,0:T(8,128)(2,1)S(1)}, u32[]{:S(2)}, u32[]{:S(2)}) collective-permute-start(bf16[1136,256]{1,0:T(8,128)(2,1)S(1)} %get-tuple-element.7.pack_ref), channel_id=1, source_target_pairs={{0,16},{16,0},{1,17},{17,1},{2,18},{18,2},{3,19},{19,3},{4,20},{20... | collective-permute-start | bytes 1744904 | tf_op jit(solution)/shard_map/ppermute | solution.py:185
  8.8 0.0 copy-done.3
  8.8 0.8 spread_queries.1
  9.6 18.9 %all-to-all-start = ((bf16[128,8,128]{2,1,0:T(8,128)(2,1)}), bf16[128,8,128]{2,1,0:T(8,128)(2,1)S(1)}, u32[]{:S(2)}, u32[]{:S(2)}) async-start(bf16[128,8,128]{2,1,0:T(8,128)(2,1)} %bitcast.1), calls=%async_computation | async-start | bytes 524288 | tf_op jit(solution)/shard_map/all_to_all | solution.py:195
  28.5 1.9 %collective-permute-start.1 = (bf16[1136,256]{1,0:T(8,128)(2,1)S(1)}, bf16[1136,256]{1,0:T(8,128)(2,1)S(1)}, u32[]{:S(2)}, u32[]{:S(2)}) collective-permute-start(bf16[1136,256]{1,0:T(8,128)(2,1)S(1)} %get-tuple-element.7.pack_ref), channel_id=1, source_target_pairs={{0,1},{1,0},{2,3},{3,2},{4,5},{5,4},{6,7},{7,6},{8,9},{9,8},{10,11... | collective-permute-start | bytes 1744904 | tf_op jit(solution)/shard_map/ppermute | solution.py:186
  30.5 0.0 collective-permute-done.far_ref
  30.5 2.4 %collective-permute-start.2 = (bf16[1136,256]{1,0:T(8,128)(2,1)S(1)}, bf16[1136,256]{1,0:T(8,128)(2,1)S(1)}, u32[]{:S(2)}, u32[]{:S(2)}) collective-permute-start(bf16[1136,256]{1,0:T(8,128)(2,1)S(1)} %collective-permute-done.far_ref), channel_id=1, source_target_pairs={{0,1},{1,0},{2,3},{3,2},{4,5},{5,4},{6,7},{7,6},{8,9},{9,8},{10,11... | collective-permute-start | bytes 1744904 | tf_op jit(solution)/shard_map/ppermute | solution.py:187
  32.9 11.7 %all-to-all-done = bf16[128,8,128]{2,1,0:T(8,128)(2,1)S(1)} async-done(((bf16[128,8,128]{2,1,0:T(8,128)(2,1)}), bf16[128,8,128]{2,1,0:T(8,128)(2,1)S(1)}, u32[]{:S(2)}, u32[]{:S(2)}) %all-to-all-start) | async-done | bytes 262176 | tf_op jit(solution)/shard_map/all_to_all | solution.py:195
  44.6 3.5 %all-to-all-start.1 = ((bf16[16,2,16,256]{3,2,1,0:T(8,128)(2,1)}), bf16[16,2,16,256]{3,2,1,0:T(8,128)(2,1)S(1)}, u32[]{:S(2)}, u32[]{:S(2)}) async-start(bf16[16,2,16,256]{3,2,1,0:T(8,128)(2,1)} %get-tuple-element.9), calls=%async_computation.1 | async-start | bytes 524288 | tf_op jit(solution)/shard_map/all_to_all | solution.py:206
  48.8 0.0 collective-permute-done.1.side_ref
  48.8 0.0 collective-permute-done.2.cross_ref
  48.8 2.8 %attend.1 = bf16[1280,128]{1,0:T(8,128)(2,1)} custom-call(s32[1]{0:T(128)S(6)} %copy.9.evict_ref, bf16[1024,128]{1,0:T(8,128)(2,1)S(1)} %bitcast.7, bf16[1136,256]{1,0:T(8,128)(2,1)S(1)} %get-tuple-element.7.pack_ref, bf16[1136,256]{1,0:T(8,128)(2,1)S(1)} %collective-permute-done.far_ref, bf16[1136,256]{1,0:T(8,128)(2,1)S(1)} %collective-permute-done.1.side_ref, ...), custom_call_target="tpu_custom_call" | custom-call | tf_op jit(solution)/shard_map/attend/pallas_call | solution.py:198
  51.6 0.0 copy-start.1
  51.6 8.2 %all-to-all-done.1.near_ref = bf16[16,2,16,256]{3,2,1,0:T(8,128)(2,1)S(1)} async-done(((bf16[16,2,16,256]{3,2,1,0:T(8,128)(2,1)}), bf16[16,2,16,256]{3,2,1,0:T(8,128)(2,1)S(1)}, u32[]{:S(2)}, u32[]{:S(2)}) %all-to-all-start.1) | async-done | bytes 262176 | tf_op jit(solution)/shard_map/all_to_all | solution.py:206
  59.9 8.0 %all-to-all-start.2 = ((bf16[640,2,128]{2,1,0:T(2,128)(2,1)}), bf16[640,2,128]{2,1,0:T(2,128)(2,1)S(1)}, u32[]{:S(2)}, u32[]{:S(2)}) async-start(bf16[640,2,128]{2,1,0:T(2,128)(2,1)} %bitcast.3), calls=%async_computation.2 | async-start | bytes 655360 | tf_op jit(solution)/shard_map/all_to_all | solution.py:208
  67.9 2.5 %collective-permute-start.3 = (bf16[16,2,16,256]{3,2,1,0:T(8,128)(2,1)S(1)}, bf16[16,2,16,256]{3,2,1,0:T(8,128)(2,1)S(1)}, u32[]{:S(2)}, u32[]{:S(2)}) collective-permute-start(bf16[16,2,16,256]{3,2,1,0:T(8,128)(2,1)S(1)} %all-to-all-done.1.near_ref), channel_id=1, source_target_pairs={{0,16},{16,0},{1,17},{17,1},{2,18},{18,2},{3,19},{19,3},{4,20},{20... | collective-permute-start | bytes 786440 | tf_op jit(solution)/shard_map/ppermute | solution.py:218
  70.4 10.2 %collective-permute-done.3.far_ref = bf16[16,2,16,256]{3,2,1,0:T(8,128)(2,1)S(1)} collective-permute-done((bf16[16,2,16,256]{3,2,1,0:T(8,128)(2,1)S(1)}, bf16[16,2,16,256]{3,2,1,0:T(8,128)(2,1)S(1)}, u32[]{:S(2)}, u32[]{:S(2)}) %collective-permute-start.3) | collective-permute-done | bytes 262176 | tf_op jit(solution)/shard_map/ppermute | solution.py:218
  80.6 0.0 copy-done.1
  80.6 0.8 renew_cache.1
  81.4 2.4 %all-to-all-done.2 = bf16[640,2,128]{2,1,0:T(2,128)(2,1)S(1)} async-done(((bf16[640,2,128]{2,1,0:T(2,128)(2,1)}), bf16[640,2,128]{2,1,0:T(2,128)(2,1)S(1)}, u32[]{:S(2)}, u32[]{:S(2)}) %all-to-all-start.2) | async-done | bytes 327712 | tf_op jit(solution)/shard_map/all_to_all | solution.py:208
  83.8 1.1 %combine.1 = bf16[2,4096]{1,0:T(2,128)(2,1)} custom-call(bf16[1280,128]{1,0:T(8,128)(2,1)S(1)} %bitcast.6), custom_call_target="tpu_custom_call" | custom-call | tf_op jit(solution)/shard_map/combine/pallas_call | solution.py:211
Async XLA Ops:
  1.3 1.0 %copy-start = (bf16[1,2,512,256]{3,2,1,0:T(8,128)(2,1)S(1)}, bf16[1,2,512,256]{3,2,1,0:T(8,128)(2,1)}, u32[]{:S(2)}) copy-start(bf16[1,2,512,256]{3,2,1,0:T(8,128)(2,1)} %cache_ref.3) | copy-start | bytes 1572868
  2.3 0.8 copy-start.2
  3.1 0.7 copy-start.4
  3.8 5.0 %copy-start.3 = (bf16[2,1,4096]{2,0,1:T(2,128)(2,1)S(1)}, bf16[2,1,4096]{2,0,1:T(2,128)(2,1)}, u32[]{:S(2)}) copy-start(bf16[2,1,4096]{2,0,1:T(2,128)(2,1)} %param.6) | copy-start | bytes 49156
  4.5 25.9 %collective-permute-start = (bf16[1136,256]{1,0:T(8,128)(2,1)S(1)}, bf16[1136,256]{1,0:T(8,128)(2,1)S(1)}, u32[]{:S(2)}, u32[]{:S(2)}) collective-permute-start(bf16[1136,256]{1,0:T(8,128)(2,1)S(1)} %get-tuple-element.7.pack_ref), channel_id=1, source_target_pairs={{0,16},{16,0},{1,17},{17,1},{2,18},{18,2},{3,19},{19,3},{4,20},{20... | collective-permute-start | bytes 1744904 | tf_op jit(solution)/shard_map/ppermute | solution.py:185
  9.6 35.0 %all-to-all-start = ((bf16[128,8,128]{2,1,0:T(8,128)(2,1)}), bf16[128,8,128]{2,1,0:T(8,128)(2,1)S(1)}, u32[]{:S(2)}, u32[]{:S(2)}) async-start(bf16[128,8,128]{2,1,0:T(8,128)(2,1)} %bitcast.1), calls=%async_computation | async-start | bytes 524288 | tf_op jit(solution)/shard_map/all_to_all | solution.py:195
  28.5 20.2 %collective-permute-start.1 = (bf16[1136,256]{1,0:T(8,128)(2,1)S(1)}, bf16[1136,256]{1,0:T(8,128)(2,1)S(1)}, u32[]{:S(2)}, u32[]{:S(2)}) collective-permute-start(bf16[1136,256]{1,0:T(8,128)(2,1)S(1)} %get-tuple-element.7.pack_ref), channel_id=1, source_target_pairs={{0,1},{1,0},{2,3},{3,2},{4,5},{5,4},{6,7},{7,6},{8,9},{9,8},{10,11... | collective-permute-start | bytes 1744904 | tf_op jit(solution)/shard_map/ppermute | solution.py:186
  30.5 18.3 %collective-permute-start.2 = (bf16[1136,256]{1,0:T(8,128)(2,1)S(1)}, bf16[1136,256]{1,0:T(8,128)(2,1)S(1)}, u32[]{:S(2)}, u32[]{:S(2)}) collective-permute-start(bf16[1136,256]{1,0:T(8,128)(2,1)S(1)} %collective-permute-done.far_ref), channel_id=1, source_target_pairs={{0,1},{1,0},{2,3},{3,2},{4,5},{5,4},{6,7},{7,6},{8,9},{9,8},{10,11... | collective-permute-start | bytes 1744904 | tf_op jit(solution)/shard_map/ppermute | solution.py:187
  44.6 15.3 %all-to-all-start.1 = ((bf16[16,2,16,256]{3,2,1,0:T(8,128)(2,1)}), bf16[16,2,16,256]{3,2,1,0:T(8,128)(2,1)S(1)}, u32[]{:S(2)}, u32[]{:S(2)}) async-start(bf16[16,2,16,256]{3,2,1,0:T(8,128)(2,1)} %get-tuple-element.9), calls=%async_computation.1 | async-start | bytes 524288 | tf_op jit(solution)/shard_map/all_to_all | solution.py:206
  51.6 29.0 %copy-start.1 = (bf16[1,2,512,256]{3,2,1,0:T(8,128)(2,1)S(1)}, bf16[1,2,512,256]{3,2,1,0:T(8,128)(2,1)}, u32[]{:S(2)}) copy-start(bf16[1,2,512,256]{3,2,1,0:T(8,128)(2,1)} %cache_ref.3) | copy-start | bytes 1572868
  59.9 23.9 %all-to-all-start.2 = ((bf16[640,2,128]{2,1,0:T(2,128)(2,1)}), bf16[640,2,128]{2,1,0:T(2,128)(2,1)S(1)}, u32[]{:S(2)}, u32[]{:S(2)}) async-start(bf16[640,2,128]{2,1,0:T(2,128)(2,1)} %bitcast.3), calls=%async_computation.2 | async-start | bytes 655360 | tf_op jit(solution)/shard_map/all_to_all | solution.py:208
  67.9 12.7 %collective-permute-start.3 = (bf16[16,2,16,256]{3,2,1,0:T(8,128)(2,1)S(1)}, bf16[16,2,16,256]{3,2,1,0:T(8,128)(2,1)S(1)}, u32[]{:S(2)}, u32[]{:S(2)}) collective-permute-start(bf16[16,2,16,256]{3,2,1,0:T(8,128)(2,1)S(1)} %all-to-all-done.1.near_ref), channel_id=1, source_target_pairs={{0,16},{16,0},{1,17},{17,1},{2,18},{18,2},{3,19},{19,3},{4,20},{20... | collective-permute-start | bytes 786440 | tf_op jit(solution)/shard_map/ppermute | solution.py:218

commit v2 on v1

--- a/solution.py
+++ b/solution.py
@@ -14,50 +14,64 @@
 NEG = -1e30
 VMEM = pl.BlockSpec(memory_space=pltpu.VMEM)
 SMEM = pl.BlockSpec(memory_space=pltpu.SMEM)
+HBM = pl.BlockSpec(memory_space=pltpu.HBM)
 NT = (((1,), (1,)), ((), ()))
 NN = (((1,), (0,)), ((), ()))
 
 
-def spread_kernel(q_ref, out_ref, rows):
-    count = rows.shape[0]
-    for row in range(count):
+def split_kernel(q_ref, out_ref, rows):
+    for row in range(rows.shape[0]):
         chip, step, head = row // PARTS, row // 4 % 2, row % 4
         start = (chip * 4 + head) * HD
         rows[row:row + 1, :] = q_ref[step:step + 1, start:start + HD].astype(jnp.float32)
-    message = rows[...].astype(out_ref.dtype)
+    out_ref[...] = rows[...].astype(out_ref.dtype)
+
+
+def spread_kernel(q_ref, clean_ref, out_ref):
+    tokens = clean_ref.shape[1]
+    count = q_ref.shape[0] + 4 * tokens
     for dest in range(out_ref.shape[0] // count):
-        out_ref[dest * count:(dest + 1) * count, :] = message
-
-
-def pack_kernel(length_ref, cache_ref, own_ref, clean_ref, pack_ref, copies_ref):
+        place = dest * count
+        out_ref[place:place + q_ref.shape[0], :] = q_ref[...]
+        place += q_ref.shape[0]
+        for half in range(2):
+            for index in range(2):
+                out_ref[place:place + tokens, :] = clean_ref[index, :, half * HD:(half + 1) * HD]
+                place += tokens
+
+
+def pack_kernel(length_ref, cache_ref, own_ref, clean_ref, pack_ref, sems):
     span, rows = cache_ref.shape[2], clean_ref.shape[1]
-    pack_ref[0:span, :] = cache_ref[0, 0]
-    pack_ref[span:2 * span, :] = cache_ref[0, 1]
-    place = 2 * span
-    for step in range(2):
-        for index in range(2):
-            pack_ref[place:place + rows, :] = own_ref[step, index]
-            place += rows
-    for index in range(2):
-        pack_ref[place:place + rows, :] = clean_ref[index]
-        place += rows
+    pieces = [(cache_ref.at[0, index], span) for index in range(2)]
+    pieces += [(own_ref.at[step, index], rows) for step in range(2) for index in range(2)]
+    pieces += [(clean_ref.at[index], rows) for index in range(2)]
+    place, copies = 0, []
+    for number, (piece, count) in enumerate(pieces):
+        copies.append(pltpu.make_async_copy(piece, pack_ref.at[pl.ds(place, count)], sems.at[number]))
+        copies[-1].start()
+        place += count
     length = length_ref[0]
     lane = lax.broadcasted_iota(jnp.int32, (rows, 2 * HD), 1)
     digits = jnp.where(lane < HD, length // 8, length % 8)
     pack_ref[place:place + rows, :] = digits.astype(jnp.float32).astype(pack_ref.dtype)
-    for dest in range(copies_ref.shape[0]):
-        copies_ref[dest] = clean_ref[...]
-
-
-def attend_kernel(evict_ref, recv_ref, pack_ref, far_ref, side_ref, cross_ref, out_ref, wide, wide_out):
-    block = recv_ref.shape[0] // PARTS
+    for copy in copies:
+        copy.wait()
+
+
+def attend_kernel(evict_ref, recv_ref, pack_ref, far_ref, side_ref, cross_ref, out_ref, clean_ref, wide, wide_out):
+    block = wide.shape[0] // PARTS
     rows = 16
     span = (pack_ref.shape[0] - 7 * rows) // 2
     tail = 2 * span
     me = lax.axis_index("ca") * 2 + lax.axis_index("cb")
     core = lax.axis_index("hb")
     owners = [me == evict_ref[0], (me ^ 1) == evict_ref[0]]
-    wide[...] = recv_ref[...].astype(jnp.float32)
+    senders = lax.axis_size("ca")
+    count, taken = recv_ref.shape[0] // senders, wide.shape[0] // senders
+    for sender in range(senders):
+        place, rest = sender * count, count - taken
+        wide[sender * taken:(sender + 1) * taken, :] = recv_ref[place:place + taken, :].astype(jnp.float32)
+        clean_ref[sender * rest:(sender + 1) * rest, :] = recv_ref[place + taken:place + count, :]
     key = lax.broadcasted_iota(jnp.int32, (1, span), 1).astype(jnp.float32)
     lane = lax.broadcasted_iota(jnp.int32, (1, HD), 1)
     lengths = []
@@ -136,7 +150,7 @@
 
 
 def renew_kernel(evict_ref, near_ref, far_ref, cache_ref, new_ref):
-    devices, _, rows, _ = near_ref.shape
+    devices, rows = lax.axis_size("ca"), 16
     parity = lax.axis_index("cb")
     owner = lax.axis_index("ca") * 2 + parity == evict_ref[0]
 
@@ -145,15 +159,17 @@
         for ref, kind in ((near_ref, parity), (far_ref, 1 - parity)):
             for device in range(devices):
                 place = pl.ds(pl.multiple_of((device * 2 + kind) * rows, rows), rows)
-                for index in range(2):
-                    new_ref[0, index, place, :] = ref[device, index]
+                for half in range(2):
+                    for index in range(2):
+                        start = ((device * 2 + half) * 2 + index) * rows
+                        new_ref[0, index, place, half * HD:(half + 1) * HD] = ref[start:start + rows, :]
 
     @pl.when(jnp.logical_not(owner))
     def _():
         new_ref[...] = cache_ref[...]
 
 
-def call(kernel, out_shape, in_specs, scratch=(), name=None):
+def call(kernel, out_shape, in_specs, scratch=(), name=None, limit=40):
     several = isinstance(out_shape, tuple)
     return pl.pallas_call(
         kernel,
@@ -161,7 +177,7 @@
         in_specs=in_specs,
         out_specs=(VMEM,) * len(out_shape) if several else VMEM,
         scratch_shapes=list(scratch),
-        compiler_params=pltpu.CompilerParams(vmem_limit_bytes=40 * 1024 * 1024),
+        compiler_params=pltpu.CompilerParams(vmem_limit_bytes=limit * 1024 * 1024),
         name=name,
     )
 
@@ -176,35 +192,36 @@
     bf16, f32 = jnp.bfloat16, jnp.float32
     shape = jax.ShapeDtypeStruct
     swap = [(0, 1), (1, 0)]
-    pack, copies = call(
+    pack = call(
         pack_kernel,
-        (shape((2 * span + 7 * rows, width), bf16), shape((pairs,) + clean_kv.shape, bf16)),
-        [SMEM] + [VMEM] * 3,
+        shape((2 * span + 7 * rows, width), bf16),
+        [SMEM] + [HBM] * 3,
+        [pltpu.SemaphoreType.DMA((8,))],
         name="pack",
+        limit=60,
     )(lengths, cache_kv, own_kv, clean_kv)
     far = lax.ppermute(pack, "cb", swap)
     side = lax.ppermute(pack, "hb", swap)
     cross = lax.ppermute(far, "hb", swap)
-    message = call(
-        spread_kernel,
-        shape((tokens * PARTS, HD), bf16),
+    split = call(
+        split_kernel,
+        shape((chips * PARTS, HD), bf16),
         [VMEM],
         [pltpu.VMEM((chips * PARTS, HD), f32)],
-        name="spread_queries",
+        name="split_queries",
     )(queries.reshape(steps, features))
-    recv = lax.all_to_all(
-        message.reshape(tokens, PARTS, HD), ("ca", "ha"), split_axis=0, concat_axis=0, tiled=True
-    ).reshape(tokens * PARTS, HD)
-    parts = call(
+    mine = lax.all_to_all(split.reshape(chips, PARTS, HD), "ha", split_axis=0, concat_axis=0, tiled=True)
+    message = call(
+        spread_kernel, shape((pairs * (chips * PARTS + 4 * rows), HD), bf16), [VMEM] * 2, name="spread"
+    )(mine.reshape(chips * PARTS, HD), clean_kv)
+    recv = lax.all_to_all(message, "ca", split_axis=0, concat_axis=0, tiled=True)
+    parts, near = call(
         attend_kernel,
-        shape((tokens * BACK, HD), bf16),
+        (shape((tokens * BACK, HD), bf16), shape((pairs * 4 * rows, HD), bf16)),
         [SMEM] + [VMEM] * 5,
         [pltpu.VMEM((tokens * PARTS, HD), f32), pltpu.VMEM((tokens * BACK, HD), f32)],
         name="attend",
     )(evict, recv, pack, far, side, cross)
-    _, copies = lax.optimization_barrier((recv, copies))
-    near = lax.all_to_all(copies, "ca", split_axis=0, concat_axis=0, tiled=True)
-    parts, near = lax.optimization_barrier((parts, near))
     back = lax.all_to_all(
         parts.reshape(tokens * BACK // 2, 2, HD), ("ca", "ha"), split_axis=0, concat_axis=0, tiled=True
     ).reshape(tokens * BACK, HD)

time: 85.5 us -> 87.6 us (1.025)
  blocking collectives: 0 us -> 22.3 us
  starting transfers between devices: 41.6 us -> 29.6 us
  waiting for transfers between devices: 32.5 us -> 25.5 us
  local copies, waits for them, and re-layouts: 2.52 us -> 0.02 us
  Pallas kernels: 6.26 us -> 7.63 us
    all_to_all x0 -> x1, blocking collectives: none -> 22.3 us  [body(): lax.all_to_all(split.reshape(chips, PARTS, HD), 'ha', split_axis=0, conca...]
    all_to_all x2 -> x1, starting transfers between devices: 22.5 us -> 9.05 us  [body(): lax.all_to_all(message, 'ca', split_axis=0, concat_axis=0, tiled=True)]
    all_to_all x2 -> x1, waiting for transfers between devices: 19.9 us -> 12.2 us  [body(): lax.all_to_all(message, 'ca', split_axis=0, concat_axis=0, tiled=True)]
    unnamed x10 -> x8, local copies, waits for them, and re-layouts: 2.52 us -> 0.02 us
    pallas_call x3 -> x4, Pallas kernels: 4.33 us -> 5.71 us  [the longest x1 2.9 us: body(): call(attend_kernel, (shape((tokens * BACK, HD), bf16), shape((pairs * 4 *...]
    all_to_all x1, starting transfers between devices: 8.04 us -> 9.14 us  [body(): lax.all_to_all(parts.reshape(tokens * BACK // 2, 2, HD), ('ca', 'ha'), sp...]
  transfers between devices with their start and end apart: 7 -> 6, of which waited for: 4 -> 3; matrix products, arithmetic and copies ran while one was open for 0% -> 0% of each run, Pallas kernels for 5% -> 2%
where the time goes in v2:
time: 87.6 us; the launch traced here: 87.1 us
  starting transfers between devices  29.6 us (34%)
  waiting for transfers between devices  25.5 us (29%)
  blocking collectives  22.3 us (25%)
  Pallas kernels  7.63 us (9%)
  between operations  2.03 us (2%)
    all_to_all x1, blocking collectives, body(): lax.all_to_all(split.reshape(chips, PARTS, HD), 'ha', split_axis=0, conca...  22.3 us
    all_to_all x1, waiting for transfers between devices, body(): lax.all_to_all(message, 'ca', split_axis=0, concat_axis=0, tiled=True)  12.2 us
    ppermute x1, waiting for transfers between devices, body(): other = lax.ppermute(near, 'cb', swap)  10.7 us
    all_to_all x1, starting transfers between devices, body(): lax.all_to_all(parts.reshape(tokens * BACK // 2, 2, HD), ('ca', 'ha'), sp...  9.14 us
    all_to_all x1, starting transfers between devices, body(): lax.all_to_all(message, 'ca', split_axis=0, concat_axis=0, tiled=True)  9.05 us
    ppermute x1, starting transfers between devices, body(): far = lax.ppermute(pack, 'cb', swap)  4.28 us
    pallas_call x1, Pallas kernels, body(): call(attend_kernel, (shape((tokens * BACK, HD), bf16), shape((pairs * 4 *...  2.9 us
    ppermute x1, starting transfers between devices, body(): other = lax.ppermute(near, 'cb', swap)  2.76 us
  transfers between devices with their start and end apart: 6, of which 3 were waited for; matrix products, arithmetic and copies ran while one was open for 0% of the time, Pallas kernels for 2%

profile of v2, /device:TPU:6, one launch (start us, length us, event | category | flops | bytes accessed | tf_op | source)
XLA Modules:
  0.0 87.1 jit_solution(7864832824249097625)
XLA Ops:
  1.3 0.0 copy-start.3
  1.3 1.9 %pack.1.pack_ref = bf16[1136,256]{1,0:T(8,128)(2,1)} custom-call(s32[1]{0:T(128)S(6)} %copy.8.length_ref, bf16[1,2,512,256]{3,2,1,0:T(8,128)(2,1)} %cache_ref.3, bf16[2,2,16,256]{3,2,1,0:T(8,128)(2,1)} %own_ref.1, bf16[2,16,256]{2,1,0:T(8,128)(2,1)} %clean_ref.3), custom_call_target="tpu_custom_call" | custom-call | tf_op jit(solution)/shard_map/pack/pallas_call | solution.py:195
  3.2 4.3 %collective-permute-start = (bf16[1136,256]{1,0:T(8,128)(2,1)}, bf16[1136,256]{1,0:T(8,128)(2,1)S(1)}, u32[]{:S(2)}, u32[]{:S(2)}) collective-permute-start(bf16[1136,256]{1,0:T(8,128)(2,1)} %pack.1.pack_ref), channel_id=1, source_target_pairs={{0,16},{16,0},{1,17},{17,1},{2,18},{18,2},{3,19},{19,3},{4,20},{20... | collective-permute-start | bytes 1744904 | tf_op jit(solution)/shard_map/ppermute | solution.py:203
  7.5 0.0 copy-done.3
  7.5 0.0 copy-start.2
  7.6 22.3 %all_to_all.21 = bf16[8,8,128]{2,1,0:T(8,128)(2,1)S(1)} all-to-all(bf16[8,8,128]{2,1,0:T(8,128)(2,1)S(1)} %bitcast.11), channel_id=1, replica_groups=mesh['ca'=16,'cb'=2,'ha'=8,'hb'=2] {'ha'}, dimensions={0} | all-to-all | bytes 32768 | tf_op jit(solution)/shard_map/all_to_all | solution.py:213
  29.8 0.0 copy-done.2
  29.8 0.9 spread.1
  30.7 0.0 copy-start
  30.7 9.0 %all-to-all-start.1 = ((bf16[16,128,128]{2,1,0:T(8,128)(2,1)}), bf16[16,128,128]{2,1,0:T(8,128)(2,1)S(1)}, u32[]{:S(2)}, u32[]{:S(2)}) async-start(bf16[16,128,128]{2,1,0:T(8,128)(2,1)} %bitcast.3), calls=%async_computation.1 | async-start | bytes 1048576 | tf_op jit(solution)/shard_map/all_to_all | solution.py:217
  39.8 0.0 copy-done
  39.8 1.9 %collective-permute-start.1 = (bf16[1136,256]{1,0:T(8,128)(2,1)S(1)}, bf16[1136,256]{1,0:T(8,128)(2,1)S(1)}, u32[]{:S(2)}, u32[]{:S(2)}) collective-permute-start(bf16[1136,256]{1,0:T(8,128)(2,1)S(1)} %copy-done), channel_id=1, source_target_pairs={{0,1},{1,0},{2,3},{3,2},{4,5},{5,4},{6,7},{7,6},{8,9},{9,8},{10,11... | collective-permute-start | bytes 1744904 | tf_op jit(solution)/shard_map/ppermute | solution.py:204
  41.7 0.0 collective-permute-done.far_ref
  41.7 2.4 %collective-permute-start.2 = (bf16[1136,256]{1,0:T(8,128)(2,1)S(1)}, bf16[1136,256]{1,0:T(8,128)(2,1)S(1)}, u32[]{:S(2)}, u32[]{:S(2)}) collective-permute-start(bf16[1136,256]{1,0:T(8,128)(2,1)S(1)} %collective-permute-done.far_ref), channel_id=1, source_target_pairs={{0,1},{1,0},{2,3},{3,2},{4,5},{5,4},{6,7},{7,6},{8,9},{9,8},{10,11... | collective-permute-start | bytes 1744904 | tf_op jit(solution)/shard_map/ppermute | solution.py:205
  44.8 0.0 collective-permute-done.1.side_ref
  44.8 12.2 %all-to-all-done.1 = bf16[16,128,128]{2,1,0:T(8,128)(2,1)S(1)} async-done(((bf16[16,128,128]{2,1,0:T(8,128)(2,1)}), bf16[16,128,128]{2,1,0:T(8,128)(2,1)S(1)}, u32[]{:S(2)}, u32[]{:S(2)}) %all-to-all-start.1) | async-done | bytes 524320 | tf_op jit(solution)/shard_map/all_to_all | solution.py:217
  57.0 0.0 collective-permute-done.2.cross_ref
  57.0 2.9 %attend.1 = (bf16[1280,128]{1,0:T(8,128)(2,1)}, bf16[1024,128]{1,0:T(8,128)(2,1)S(1)}) custom-call(s32[1]{0:T(128)S(6)} %copy.9.evict_ref, bf16[2048,128]{1,0:T(8,128)(2,1)S(1)} %bitcast.8, bf16[1136,256]{1,0:T(8,128)(2,1)S(1)} %copy-done, bf16[1136,256]{1,0:T(8,128)(2,1)S(1)} %collective-permute-done.far_ref, ...), custom_call_target="tpu_custom_call" | custom-call | tf_op jit(solution)/shard_map/attend/pallas_call | solution.py:218
  59.9 0.0 copy-start.1
  59.9 9.1 %all-to-all-start.2 = ((bf16[640,2,128]{2,1,0:T(2,128)(2,1)}), bf16[640,2,128]{2,1,0:T(2,128)(2,1)S(1)}, u32[]{:S(2)}, u32[]{:S(2)}) async-start(bf16[640,2,128]{2,1,0:T(2,128)(2,1)} %bitcast.5), calls=%async_computation.2 | async-start | bytes 655360 | tf_op jit(solution)/shard_map/all_to_all | solution.py:225
  69.0 2.8 %collective-permute-start.3 = (bf16[1024,128]{1,0:T(8,128)(2,1)S(1)}, bf16[1024,128]{1,0:T(8,128)(2,1)S(1)}, u32[]{:S(2)}, u32[]{:S(2)}) collective-permute-start(bf16[1024,128]{1,0:T(8,128)(2,1)S(1)} %get-tuple-element.5.near_ref), channel_id=1, source_target_pairs={{0,16},{16,0},{1,17},{17,1},{2,18},{18,2},{3,19},{19,3},{4,20},{20... | collective-permute-start | bytes 786440 | tf_op jit(solution)/shard_map/ppermute | solution.py:235
  71.8 10.7 %collective-permute-done.3.far_ref = bf16[1024,128]{1,0:T(8,128)(2,1)S(1)} collective-permute-done((bf16[1024,128]{1,0:T(8,128)(2,1)S(1)}, bf16[1024,128]{1,0:T(8,128)(2,1)S(1)}, u32[]{:S(2)}, u32[]{:S(2)}) %collective-permute-start.3) | collective-permute-done | bytes 262176 | tf_op jit(solution)/shard_map/ppermute | solution.py:235
  82.5 0.0 copy-done.1
  82.5 0.8 renew_cache.1
  83.4 2.6 %all-to-all-done.2 = bf16[640,2,128]{2,1,0:T(2,128)(2,1)S(1)} async-done(((bf16[640,2,128]{2,1,0:T(2,128)(2,1)}), bf16[640,2,128]{2,1,0:T(2,128)(2,1)S(1)}, u32[]{:S(2)}, u32[]{:S(2)}) %all-to-all-start.2) | async-done | bytes 327712 | tf_op jit(solution)/shard_map/all_to_all | solution.py:225
  86.0 1.1 %combine.1 = bf16[2,4096]{1,0:T(2,128)(2,1)} custom-call(bf16[1280,128]{1,0:T(8,128)(2,1)S(1)} %bitcast.9), custom_call_target="tpu_custom_call" | custom-call | tf_op jit(solution)/shard_map/combine/pallas_call | solution.py:228
  (1 shorter events, 0.0 us)
Async XLA Ops:
  1.3 6.2 %copy-start.3 = (bf16[2,1,4096]{2,0,1:T(2,128)(2,1)S(1)}, bf16[2,1,4096]{2,0,1:T(2,128)(2,1)}, u32[]{:S(2)}) copy-start(bf16[2,1,4096]{2,0,1:T(2,128)(2,1)} %param.6) | copy-start | bytes 49156
  3.2 38.5 %collective-permute-start = (bf16[1136,256]{1,0:T(8,128)(2,1)}, bf16[1136,256]{1,0:T(8,128)(2,1)S(1)}, u32[]{:S(2)}, u32[]{:S(2)}) collective-permute-start(bf16[1136,256]{1,0:T(8,128)(2,1)} %pack.1.pack_ref), channel_id=1, source_target_pairs={{0,16},{16,0},{1,17},{17,1},{2,18},{18,2},{3,19},{19,3},{4,20},{20... | collective-permute-start | bytes 1744904 | tf_op jit(solution)/shard_map/ppermute | solution.py:203
  7.5 22.3 %copy-start.2 = (bf16[2,16,256]{2,1,0:T(8,128)(2,1)S(1)}, bf16[2,16,256]{2,1,0:T(8,128)(2,1)}, u32[]{:S(2)}) copy-start(bf16[2,16,256]{2,1,0:T(8,128)(2,1)} %clean_ref.3) | copy-start | bytes 49156
  30.7 9.1 %copy-start = (bf16[1136,256]{1,0:T(8,128)(2,1)S(1)}, bf16[1136,256]{1,0:T(8,128)(2,1)}, u32[]{:S(2)}) copy-start(bf16[1136,256]{1,0:T(8,128)(2,1)} %pack.1.pack_ref) | copy-start | bytes 1744900
  30.7 26.3 %all-to-all-start.1 = ((bf16[16,128,128]{2,1,0:T(8,128)(2,1)}), bf16[16,128,128]{2,1,0:T(8,128)(2,1)S(1)}, u32[]{:S(2)}, u32[]{:S(2)}) async-start(bf16[16,128,128]{2,1,0:T(8,128)(2,1)} %bitcast.3), calls=%async_computation.1 | async-start | bytes 1048576 | tf_op jit(solution)/shard_map/all_to_all | solution.py:217
  39.8 5.0 %collective-permute-start.1 = (bf16[1136,256]{1,0:T(8,128)(2,1)S(1)}, bf16[1136,256]{1,0:T(8,128)(2,1)S(1)}, u32[]{:S(2)}, u32[]{:S(2)}) collective-permute-start(bf16[1136,256]{1,0:T(8,128)(2,1)S(1)} %copy-done), channel_id=1, source_target_pairs={{0,1},{1,0},{2,3},{3,2},{4,5},{5,4},{6,7},{7,6},{8,9},{9,8},{10,11... | collective-permute-start | bytes 1744904 | tf_op jit(solution)/shard_map/ppermute | solution.py:204
  41.7 15.3 %collective-permute-start.2 = (bf16[1136,256]{1,0:T(8,128)(2,1)S(1)}, bf16[1136,256]{1,0:T(8,128)(2,1)S(1)}, u32[]{:S(2)}, u32[]{:S(2)}) collective-permute-start(bf16[1136,256]{1,0:T(8,128)(2,1)S(1)} %collective-permute-done.far_ref), channel_id=1, source_target_pairs={{0,1},{1,0},{2,3},{3,2},{4,5},{5,4},{6,7},{7,6},{8,9},{9,8},{10,11... | collective-permute-start | bytes 1744904 | tf_op jit(solution)/shard_map/ppermute | solution.py:205
  59.9 22.7 %copy-start.1 = (bf16[1,2,512,256]{3,2,1,0:T(8,128)(2,1)S(1)}, bf16[1,2,512,256]{3,2,1,0:T(8,128)(2,1)}, u32[]{:S(2)}) copy-start(bf16[1,2,512,256]{3,2,1,0:T(8,128)(2,1)} %cache_ref.3) | copy-start | bytes 1572868
  59.9 26.1 %all-to-all-start.2 = ((bf16[640,2,128]{2,1,0:T(2,128)(2,1)}), bf16[640,2,128]{2,1,0:T(2,128)(2,1)S(1)}, u32[]{:S(2)}, u32[]{:S(2)}) async-start(bf16[640,2,128]{2,1,0:T(2,128)(2,1)} %bitcast.5), calls=%async_computation.2 | async-start | bytes 655360 | tf_op jit(solution)/shard_map/all_to_all | solution.py:225
  69.0 13.5 %collective-permute-start.3 = (bf16[1024,128]{1,0:T(8,128)(2,1)S(1)}, bf16[1024,128]{1,0:T(8,128)(2,1)S(1)}, u32[]{:S(2)}, u32[]{:S(2)}) collective-permute-start(bf16[1024,128]{1,0:T(8,128)(2,1)S(1)} %get-tuple-element.5.near_ref), channel_id=1, source_target_pairs={{0,16},{16,0},{1,17},{17,1},{2,18},{18,2},{3,19},{19,3},{4,20},{20... | collective-permute-start | bytes 786440 | tf_op jit(solution)/shard_map/ppermute | solution.py:235
